TPU v7x, 32 devices: a whole 2x2x4 slice. The times are simulated.
32 devices in a mesh: rows: 16 (over z, y, core), rep: 2 (over x).
Axes of the slice: x: 2, y: 2, z: 4, core: 2. Of those that a mesh axis runs over, the one named last changes fastest.
Arguments:
- embeddings: bfloat16 [11264, 1024], P(('rows', 'rep')), may hold values from -6 to 6
- owner_ids: int32 [11264, 1], P(('rows', 'rep')), may hold values from 0 to 15; in each aligned block of 352 rows (0 to 351, 352 to 703, ...) at most 64 rows name the same one
- live_mask: int32 [11264], P(('rows', 'rep')), may hold values 0 or 1
Outputs:
- neighbour_means: bfloat16 [11264, 1024], P(('rows', 'rep'))
Inputs may be any that keep to these rules, and one draw needn't show every extreme that they name: `owner_ids`: among the rows of one device, at most 64 name the same owner, and in every draw some owner is named by exactly 64 of them.
All inputs are finite; a program needn't handle non-finite values. Where the computation divides by a largest or mean magnitude, that divisor is 1e-20 or more. No bound on the sum of `live_mask` on one device may be relied on, other than what follows from the above.
Results may differ from a plain program's by a relative error of at most 0.0017.
The roundings to bfloat16 on the way count: a program that leaves them out, or rounds other values in their place, can miss the bound.
Values may be sent and summed in bfloat16 or wider, within the bound.
A program may use at most 64 MiB of HBM per device.

v0:
```python
import jax
import jax.numpy as jnp
from jax import lax
from jax.sharding import PartitionSpec as P

BUCKET = 1024
JOIN_ROWS = 8192
KERNEL_SCALE = 4.0
EPSILON = 1e-06
SPLIT = lax.Precision.HIGH
PRECISE = lax.Precision.HIGHEST


def block_positions(owner_block, owners, slot_cap):
    rows = owner_block.shape[0]
    same = owner_block[:, None] == owner_block[None, :]
    index = jnp.arange(rows, dtype=jnp.int32)
    earlier = index[None, :] < index[:, None]
    slot_rank = jnp.sum((same & earlier).astype(jnp.int32), axis=1)
    return owner_block * slot_cap + slot_rank


def whiten(embedded, inverse_root):
    mapped = jnp.dot(embedded, inverse_root, preferred_element_type=jnp.float32)
    return (mapped * lax.rsqrt(jnp.mean(mapped * mapped, axis=1, keepdims=True) + EPSILON)).astype(
        jnp.bfloat16
    )


def root_of(moment):
    y = moment / jnp.max(jnp.sum(jnp.abs(moment), axis=1))
    eye = jnp.eye(y.shape[0], dtype=jnp.float32)
    square = jnp.dot(y, y, precision=SPLIT)
    inner = 1.6875 * eye - 0.5625 * y + 0.0625 * square
    return (2.25 * eye - 2.4375 * y + jnp.dot(square, inner, precision=SPLIT)).astype(jnp.bfloat16)


def masked_means(queries, members, same, alive):
    scores = lax.dot_general(
        queries, members, (((1,), (1,)), ((), ())), preferred_element_type=jnp.float32
    )
    weights = jnp.where(same, jnp.exp(KERNEL_SCALE * (scores / members.shape[1] - 1.0)), 0.0)
    denominator = jnp.sum(weights, axis=1, keepdims=True)
    summed = jnp.dot(weights.astype(jnp.bfloat16), members, preferred_element_type=jnp.float32)
    averaged = summed / jnp.where(alive[:, None] > 0, denominator, 1.0)
    normed = averaged * lax.rsqrt(jnp.mean(averaged * averaged, axis=1, keepdims=True) + EPSILON)
    return (normed * alive[:, None]).astype(jnp.bfloat16)


def spread(values, positions, slots_all):
    return jnp.zeros((slots_all,) + values.shape[1:], values.dtype).at[positions].set(values)


def by_exchange(embeddings, owner_ids, live_mask):
    rows_here, columns = embeddings.shape
    owners = lax.axis_size("rows")
    slot_cap = BUCKET // owners
    positions = block_positions(owner_ids[:, 0], owners, slot_cap)
    live_rows = live_mask.astype(jnp.bfloat16)
    masked = embeddings * live_rows[:, None]
    partial_moment = lax.dot_general(
        masked, masked, (((0,), (0,)), ((), ())), preferred_element_type=jnp.float32
    )
    inverse_root = root_of(lax.psum(partial_moment, ("rows", "rep")))
    whitened = whiten(embeddings, inverse_root)

    def swapped(values):
        return lax.all_to_all(values, "rows", split_axis=0, concat_axis=0, tiled=True)

    members = swapped(
        spread(whitened, positions, BUCKET).reshape(owners, slot_cap, columns)
    ).reshape(BUCKET, columns)
    alive = swapped(spread(live_rows, positions, BUCKET).reshape(owners, slot_cap))
    alive = alive.reshape(BUCKET).astype(jnp.float32)
    means = masked_means(members, members, alive[None, :] > 0, alive)
    returned = swapped(means.reshape(owners, slot_cap, columns))
    return returned.reshape(BUCKET, columns)[positions]


def by_gather(embeddings, owner_ids, live_mask):
    rows_here, columns = embeddings.shape
    owners = lax.axis_size("rows")
    key = jnp.where(live_mask > 0, owner_ids[:, 0], -1)
    keys = lax.all_gather(key, "rows", axis=0, tiled=True)
    everyone = lax.all_gather(embeddings, "rows", axis=0, tiled=True)
    share = columns // owners
    masked = everyone * (keys >= 0).astype(jnp.bfloat16)[:, None]
    own = lax.dynamic_slice_in_dim(masked, lax.axis_index("rows") * share, share, 1)
    part = lax.dot_general(
        own, masked, (((0,), (0,)), ((), ())), preferred_element_type=jnp.float32
    )
    part = lax.psum(part, "rep")
    moment = lax.all_gather(part, "rows", axis=0, tiled=True)
    whitened = whiten(everyone, root_of(moment))
    mine = lax.dynamic_slice_in_dim(whitened, lax.axis_index("rows") * rows_here, rows_here, 0)
    alive = (live_mask > 0).astype(jnp.float32)
    return masked_means(mine, whitened, owner_ids == keys[None, :], alive)


def solution(mesh):
    placed = (P(("rows", "rep"), None), P(("rows", "rep"), None), P(("rows", "rep")))

    def per_device(embeddings, owner_ids, live_mask):
        gathered = embeddings.shape[0] * mesh.shape["rows"]
        join = by_gather if gathered <= JOIN_ROWS else by_exchange
        return join(embeddings, owner_ids, live_mask)

    return jax.shard_map(
        per_device, mesh=mesh, in_specs=placed, out_specs=P(("rows", "rep"), None), check_vma=False
    )
```

profile of v0, /device:TPU:0, one launch (start us, length us, event | category | flops | bytes accessed | tf_op | source)
XLA Modules:
  0.0 265.8 jit_solution(3059865663002023440)
XLA Ops:
  6.5 0.7 all-gather.3.cloned.1.call-update
  7.3 0.0 all-reduce.3.cloned.1.call-start
  7.3 0.7 reduce.1
  8.0 1.2 dynamic-slice.4
  9.9 0.7 fusion.31
  10.6 0.1 select_dynamic-update-slice_fusion
  10.7 65.3 %all-reduce = s32[5632]{0:T(1024)S(1)} all-reduce(s32[5632]{0:T(1024)S(1)} %select_dynamic-update-slice_fusion), channel_id=1, replica_groups=mesh['rows'=16,'rep'=2] {'rows'}, use_global_device_ids=true, to_apply=%add | all-reduce | flops 5632 | bytes 45056
  76.0 31.2 %all-gather.3.cloned.1.call-done = bf16[5632,1024]{1,0:T(8,128)(2,1)} async-done(((bf16[352,1024]{1,0:T(8,128)(2,1)}), bf16[5632,1024]{1,0:T(8,128)(2,1)}) %all-gather.3.cloned.1.call-update) | async-done | bytes 11534352 | tf_op jit(solution)/shard_map/all_gather | solution.py:85
  107.2 7.0 %broadcast_multiply_fusion = bf16[5632,1024]{1,0:T(8,128)(2,1)S(1)} fusion(bf16[5632,1024]{1,0:T(8,128)(2,1)} %all-gather.3.cloned.1.call-done, bf16[5632]{0:T(1024)(128)(2,1)S(1)} %compare_convert_fusion), kind=kLoop, calls=%fused_computation.7 | loop fusion | flops 5767168 | bytes 23079936 | tf_op jit(solution)/shard_map/mul | solution.py:87
  114.2 3.3 %fusion.19 = f32[64,1024]{1,0:T(8,128)} fusion(bf16[5632,1024]{1,0:T(8,128)(2,1)S(1)} %broadcast_multiply_fusion, s32[]{:T(128)S(6)} %select_n.20), kind=kOutput, calls=%fused_computation.27 | convolution fusion | flops 738197504 | bytes 13238276 | tf_op jit(solution)/shard_map/dot_general | solution.py:89
  117.5 0.0 all-reduce.3.cloned.1.call-update
  117.5 0.0 all-gather.5.cloned.1.call-start
  117.6 21.7 %all-reduce.3.cloned.1.call-done = f32[64,1024]{1,0:T(8,128)} async-done(((f32[64,1024]{1,0:T(8,128)}), f32[64,1024]{1,0:T(8,128)}) %all-reduce.3.cloned.1.call-update) | async-done | bytes 262160 | tf_op jit(solution)/shard_map/psum | solution.py:92
  139.3 0.0 all-gather.5.cloned.1.call-update
  139.3 53.0 %all-gather.5.cloned.1.call-done = f32[1024,1024]{1,0:T(8,128)} async-done(((f32[64,1024]{1,0:T(8,128)}), f32[1024,1024]{1,0:T(8,128)}) %all-gather.5.cloned.1.call-update) | async-done | bytes 4194320 | tf_op jit(solution)/shard_map/all_gather | solution.py:93
  192.3 2.6 abs_reduce_fusion
  194.8 0.6 reduce_max.9
  195.4 11.7 %fusion.18 = f32[1024,1024]{1,0:T(8,128)S(1)} fusion(f32[1024,1024]{1,0:T(8,128)} %all-gather.5.cloned.1.call-done, f32[]{:T(128)} %reduce_max.9), kind=kOutput, calls=%fused_computation.24 | convolution fusion | flops 6443499520 | bytes 8388612 | tf_op jit(solution)/shard_map/dot_general | solution.py:33
  207.2 8.6 %add_convert_fusion = bf16[1024,1024]{1,0:T(8,128)(2,1)S(1)} fusion(f32[1024,1024]{1,0:T(8,128)S(1)} %fusion.18, f32[1024,1024]{1,0:T(8,128)S(1)} %copy-done, f32[]{:T(128)} %reduce_max.9), kind=kOutput, calls=%fused_computation.8 | convolution fusion | flops 6457131008 | bytes 10485764 | tf_op jit(solution)/shard_map/dot_general | solution.py:35
  215.8 19.5 %multiply_reduce_fusion = (f32[5632]{0:T(1024)S(1)}, f32[1024,5632]{1,0:T(8,128)}) fusion(bf16[1024,1024]{1,0:T(8,128)(2,1)S(1)} %add_convert_fusion, bf16[5632,1024]{1,0:T(8,128)(2,1)} %all-gather.3.cloned.1.call-done), kind=kOutput, calls=%fused_computation.1 | convolution fusion | flops 11822688256 | bytes 36722688 | tf_op jit(solution)/shard_map/dot_general | solution.py:24
  235.3 8.7 %multiply_convert_fusion = bf16[1024,5632]{1,0:T(8,128)(2,1)S(1)} fusion(f32[1024,5632]{1,0:T(8,128)} %get-tuple-element.8, f32[5632]{0:T(1024)S(1)} %add_rsqrt_fusion), kind=kLoop, calls=%fused_computation | loop fusion | flops 11534336 | bytes 34625536 | tf_op jit(solution)/shard_map/convert_element_type | solution.py:25
  244.0 7.7 %fusion.32 = (f32[352]{0:T(512)S(1)}, bf16[352,5632]{1,0:T(8,128)(2,1)}) fusion(bf16[1024,5632]{1,0:T(8,128)(2,1)S(1)} %multiply_convert_fusion, s32[]{:T(128)S(6)} %select_n.21, s32[5632]{0:T(1024)S(1)} %all-reduce, s32[352]{0:T(512)S(1)} %reduce.1), kind=kOutput, calls=%fused_computation.44 | convolution fusion | flops 4073963264 | bytes 16313732 | tf_op jit(solution)/shard_map/dot_general | solution.py:39
  251.7 6.5 %multiply_reduce_fusion.1 = (f32[352]{0:T(512)S(1)}, f32[352,1024]{1,0:T(8,128)S(1)}) fusion(f32[352]{0:T(512)S(1)} %compare_select_fusion, bf16[1024,5632]{1,0:T(8,128)(2,1)S(1)} %multiply_convert_fusion, bf16[352,5632]{1,0:T(8,128)(2,1)} %get-tuple-element.10), kind=kOutput, calls=%fused_computation.26 | convolution fusion | flops 4061167360 | bytes 16943872 | tf_op jit(solution)/shard_map/dot_general | solution.py:44
  258.2 1.1 multiply_convert_fusion.1
  (8 shorter events, 0.0 us)
Async XLA Ops:
  6.5 100.7 %all-gather.3.cloned.1.call-start = ((), (), s32[]{:S(2)}) async-start(), calls=%async_computation | async-start | bytes 12255232 | tf_op jit(solution)/shard_map/all_gather | solution.py:85
  7.3 132.0 %all-reduce.3.cloned.1.call-start = ((), (), s32[]{:S(2)}) async-start(), calls=%async_computation.1 | async-start | bytes 524288 | tf_op jit(solution)/shard_map/psum | solution.py:92
  117.5 74.8 %all-gather.5.cloned.1.call-start = ((), (), s32[]{:S(2)}) async-start(), calls=%async_computation.2 | async-start | bytes 4456448 | tf_op jit(solution)/shard_map/all_gather | solution.py:93
  195.4 11.7 %copy-start = (f32[1024,1024]{1,0:T(8,128)S(1)}, f32[1024,1024]{1,0:T(8,128)}, u32[]{:S(2)}) copy-start(f32[1024,1024]{1,0:T(8,128)} %all-gather.5.cloned.1.call-done) | copy-start | bytes 12582916
Sparse Core Ops, SparseCore 0:
  9.6 97.5 all-gather.2
  117.6 21.6 all-reduce.2
  141.7 50.5 all-gather.4
where the time goes:
time: 266 us
  waiting for transfers between devices  107 us (40%)
  blocking collectives  65.3 us (25%)
  matrix products  57.3 us (22%)
  other arithmetic  21.4 us (8%)
  between operations  13.8 us (5%)
    unnamed x1, blocking collectives  65.3 us
    all_gather x1, waiting for transfers between devices, by_gather(): moment = lax.all_gather(part, 'rows', axis=0, tiled=True)  53 us
    all_gather x1, waiting for transfers between devices, by_gather(): everyone = lax.all_gather(embeddings, 'rows', axis=0, tiled=True)  31.2 us
    psum x1, waiting for transfers between devices, by_gather(): part = lax.psum(part, 'rep')  21.7 us
    dot_general x1, matrix products, whiten(): mapped = jnp.dot(embedded, inverse_root, preferred_element_type=jnp.float32)  19.5 us
    dot_general x1, matrix products, root_of(): square = jnp.dot(y, y, precision=SPLIT)  11.7 us
    convert_element_type x1, other arithmetic, whiten(): (mapped * lax.rsqrt(jnp.mean(mapped * mapped, axis=1, keepdims=True) + EP...  8.69 us
    dot_general x1, matrix products, root_of(): jnp.dot(square, inner, precision=SPLIT)  8.6 us
  transfers between devices with their start and end apart: 3, of which 3 were waited for; matrix products, arithmetic and copies ran while one was open for 1% of the time, Pallas kernels for 0%

commit v1 on v0

--- a/solution.py
+++ b/solution.py
@@ -90,7 +90,30 @@
         own, masked, (((0,), (0,)), ((), ())), preferred_element_type=jnp.float32
     )
     part = lax.psum(part, "rep")
-    moment = lax.all_gather(part, "rows", axis=0, tiled=True)
+    known, carry, opened = (lax.axis_size("rows"), lax.axis_index("rows"), part.shape[0])
+    formed = local_now = part
+    moment = lax.dynamic_update_slice_in_dim(
+        jnp.zeros(
+            tuple((dd * known if kk == 0 else dd for kk, dd in enumerate(part.shape))), part.dtype
+        ),
+        part,
+        carry * opened,
+        axis=0,
+    )
+    for num in tuple(range(1, known // 2 + 1)):
+        formed = lax.ppermute(
+            formed, "rows", tuple(((kk, (kk + 1) % known) for kk in range(known)))
+        )
+        moment = lax.dynamic_update_slice_in_dim(
+            moment, formed, (carry - num) % known * opened, axis=0
+        )
+        if 2 * num < known:
+            local_now = lax.ppermute(
+                local_now, "rows", tuple(((kk, (kk - 1) % known) for kk in range(known)))
+            )
+            moment = lax.dynamic_update_slice_in_dim(
+                moment, local_now, (carry + num) % known * opened, axis=0
+            )
     whitened = whiten(everyone, root_of(moment))
     mine = lax.dynamic_slice_in_dim(whitened, lax.axis_index("rows") * rows_here, rows_here, 0)
     alive = (live_mask > 0).astype(jnp.float32)

time: 266 us -> 282 us (1.060)
  starting transfers between devices: 0.08 us -> 32 us
  waiting for transfers between devices: 107 us -> 89.8 us
    all_gather x1 -> x0, waiting for transfers between devices: 53 us -> none  [by_gather(): moment = lax.all_gather(part, 'rows', axis=0, tiled=True)]
    ppermute x0 -> x15, waiting for transfers between devices: none -> 36 us  [the longest x8 34.6 us: by_gather(): lax.ppermute(formed, 'rows', tuple(((kk, (kk + 1) % known) for kk in rang...]
    ppermute x0 -> x15, starting transfers between devices: none -> 32 us  [the longest x7 31.9 us: by_gather(): lax.ppermute(local_now, 'rows', tuple(((kk, (kk - 1) % known) for kk in r...]
  transfers between devices with their start and end apart: 3 -> 17, of which waited for: 3 -> 14; matrix products, arithmetic and copies ran while one was open for 1% -> 1% of each run, Pallas kernels for 0% -> 0%
where the time goes in v1:
time: 282 us
  waiting for transfers between devices  89.8 us (32%)
  blocking collectives  65.2 us (23%)
  matrix products  57.5 us (20%)
  starting transfers between devices  32 us (11%)
  other arithmetic  19.2 us (7%)
  between operations  14.2 us (5%)
  local copies, waits for them, and re-layouts  4.05 us (1%)
    unnamed x1, blocking collectives  65.2 us
    ppermute x8, waiting for transfers between devices, by_gather(): lax.ppermute(formed, 'rows', tuple(((kk, (kk + 1) % known) for kk in rang...  34.6 us
    ppermute x7, starting transfers between devices, by_gather(): lax.ppermute(local_now, 'rows', tuple(((kk, (kk - 1) % known) for kk in r...  31.9 us
    all_gather x1, waiting for transfers between devices, by_gather(): everyone = lax.all_gather(embeddings, 'rows', axis=0, tiled=True)  31.4 us
    psum x1, waiting for transfers between devices, by_gather(): part = lax.psum(part, 'rep')  21.8 us
    dot_general x1, matrix products, whiten(): mapped = jnp.dot(embedded, inverse_root, preferred_element_type=jnp.float32)  19.6 us
    dot_general x1, matrix products, root_of(): square = jnp.dot(y, y, precision=SPLIT)  11.7 us
    convert_element_type x1, other arithmetic, whiten(): (mapped * lax.rsqrt(jnp.mean(mapped * mapped, axis=1, keepdims=True) + EP...  8.69 us
  transfers between devices with their start and end apart: 17, of which 14 were waited for; matrix products, arithmetic and copies ran while one was open for 1% of the time, Pallas kernels for 0%

profile of v1, /device:TPU:0, one launch (start us, length us, event | category | flops | bytes accessed | tf_op | source)
XLA Modules:
  0.0 282.0 jit_solution(8569070241585897082)
XLA Ops:
  10.7 65.2 %all-reduce = s32[5632]{0:T(1024)S(1)} all-reduce(s32[5632]{0:T(1024)S(1)} %select_dynamic-update-slice_fusion), channel_id=1, replica_groups=mesh['rows'=16,'rep'=2] {'rows'}, use_global_device_ids=true, to_apply=%add | all-reduce | flops 5632 | bytes 45056
  75.9 31.4 %all-gather.2.cloned.1.call-done = bf16[5632,1024]{1,0:T(8,128)(2,1)} async-done(((bf16[352,1024]{1,0:T(8,128)(2,1)}), bf16[5632,1024]{1,0:T(8,128)(2,1)}) %all-gather.2.cloned.1.call-update) | async-done | bytes 11534352 | tf_op jit(solution)/shard_map/all_gather | solution.py:85
  107.2 7.0 %broadcast_multiply_fusion = bf16[5632,1024]{1,0:T(8,128)(2,1)S(1)} fusion(bf16[5632,1024]{1,0:T(8,128)(2,1)} %all-gather.2.cloned.1.call-done, bf16[5632]{0:T(1024)(128)(2,1)S(1)} %compare_convert_fusion), kind=kLoop, calls=%fused_computation.7 | loop fusion | flops 5767168 | bytes 23079936 | tf_op jit(solution)/shard_map/mul | solution.py:87
  117.5 21.8 %all-reduce.3.cloned.1.call-done = f32[64,1024]{1,0:T(8,128)} async-done(((f32[64,1024]{1,0:T(8,128)}), f32[64,1024]{1,0:T(8,128)}) %all-reduce.3.cloned.1.call-update) | async-done | bytes 262160 | tf_op jit(solution)/shard_map/psum | solution.py:92
  139.3 4.4 %collective-permute-start.1 = (f32[64,1024]{1,0:T(8,128)}, f32[64,1024]{1,0:T(8,128)S(1)}, u32[]{:S(2)}, u32[]{:S(2)}) collective-permute-start(f32[64,1024]{1,0:T(8,128)} %all-reduce.3.cloned.1.call-done), channel_id=1, source_target_pairs={{0,30},{2,0},{4,2},{6,4},{8,6},{10,8},{12,10},{14,12},{16,14},{18,... | collective-permute-start | bytes 786440 | tf_op jit(solution)/shard_map/ppermute | solution.py:111
  143.7 4.4 %collective-permute-done = f32[64,1024]{1,0:T(8,128)S(1)} collective-permute-done((f32[64,1024]{1,0:T(8,128)}, f32[64,1024]{1,0:T(8,128)S(1)}, u32[]{:S(2)}, u32[]{:S(2)}) %collective-permute-start) | collective-permute-done | bytes 262176 | tf_op jit(solution)/shard_map/ppermute | solution.py:104
  148.1 4.4 %collective-permute-start.3 = (f32[64,1024]{1,0:T(8,128)S(1)}, f32[64,1024]{1,0:T(8,128)S(1)}, u32[]{:S(2)}, u32[]{:S(2)}) collective-permute-start(f32[64,1024]{1,0:T(8,128)S(1)} %collective-permute-done.1), channel_id=1, source_target_pairs={{0,30},{2,0},{4,2},{6,4},{8,6},{10,8},{12,10},{14,12},{16,14},{18,... | collective-permute-start | bytes 786440 | tf_op jit(solution)/shard_map/ppermute | solution.py:111
  152.5 4.2 %collective-permute-done.2 = f32[64,1024]{1,0:T(8,128)S(1)} collective-permute-done((f32[64,1024]{1,0:T(8,128)S(1)}, f32[64,1024]{1,0:T(8,128)S(1)}, u32[]{:S(2)}, u32[]{:S(2)}) %collective-permute-start.2) | collective-permute-done | bytes 262176 | tf_op jit(solution)/shard_map/ppermute | solution.py:104
  156.7 4.4 %collective-permute-start.5 = (f32[64,1024]{1,0:T(8,128)S(1)}, f32[64,1024]{1,0:T(8,128)S(1)}, u32[]{:S(2)}, u32[]{:S(2)}) collective-permute-start(f32[64,1024]{1,0:T(8,128)S(1)} %collective-permute-done.3), channel_id=1, source_target_pairs={{0,30},{2,0},{4,2},{6,4},{8,6},{10,8},{12,10},{14,12},{16,14},{18,... | collective-permute-start | bytes 786440 | tf_op jit(solution)/shard_map/ppermute | solution.py:111
  161.1 4.2 %collective-permute-done.4 = f32[64,1024]{1,0:T(8,128)S(1)} collective-permute-done((f32[64,1024]{1,0:T(8,128)S(1)}, f32[64,1024]{1,0:T(8,128)S(1)}, u32[]{:S(2)}, u32[]{:S(2)}) %collective-permute-start.4) | collective-permute-done | bytes 262176 | tf_op jit(solution)/shard_map/ppermute | solution.py:104
  165.9 4.5 %collective-permute-start.7 = (f32[64,1024]{1,0:T(8,128)S(1)}, f32[64,1024]{1,0:T(8,128)S(1)}, u32[]{:S(2)}, u32[]{:S(2)}) collective-permute-start(f32[64,1024]{1,0:T(8,128)S(1)} %collective-permute-done.5), channel_id=1, source_target_pairs={{0,30},{2,0},{4,2},{6,4},{8,6},{10,8},{12,10},{14,12},{16,14},{18,... | collective-permute-start | bytes 786440 | tf_op jit(solution)/shard_map/ppermute | solution.py:111
  170.4 3.5 %collective-permute-done.6 = f32[64,1024]{1,0:T(8,128)S(1)} collective-permute-done((f32[64,1024]{1,0:T(8,128)S(1)}, f32[64,1024]{1,0:T(8,128)S(1)}, u32[]{:S(2)}, u32[]{:S(2)}) %collective-permute-start.6) | collective-permute-done | bytes 262176 | tf_op jit(solution)/shard_map/ppermute | solution.py:104
  174.3 4.7 %collective-permute-start.9 = (f32[64,1024]{1,0:T(8,128)S(1)}, f32[64,1024]{1,0:T(8,128)S(1)}, u32[]{:S(2)}, u32[]{:S(2)}) collective-permute-start(f32[64,1024]{1,0:T(8,128)S(1)} %collective-permute-done.7), channel_id=1, source_target_pairs={{0,30},{2,0},{4,2},{6,4},{8,6},{10,8},{12,10},{14,12},{16,14},{18,... | collective-permute-start | bytes 786440 | tf_op jit(solution)/shard_map/ppermute | solution.py:111
  179.0 3.5 %collective-permute-done.8 = f32[64,1024]{1,0:T(8,128)S(1)} collective-permute-done((f32[64,1024]{1,0:T(8,128)S(1)}, f32[64,1024]{1,0:T(8,128)S(1)}, u32[]{:S(2)}, u32[]{:S(2)}) %collective-permute-start.8) | collective-permute-done | bytes 262176 | tf_op jit(solution)/shard_map/ppermute | solution.py:104
  182.9 4.7 %collective-permute-start.11 = (f32[64,1024]{1,0:T(8,128)S(1)}, f32[64,1024]{1,0:T(8,128)S(1)}, u32[]{:S(2)}, u32[]{:S(2)}) collective-permute-start(f32[64,1024]{1,0:T(8,128)S(1)} %collective-permute-done.9), channel_id=1, source_target_pairs={{0,30},{2,0},{4,2},{6,4},{8,6},{10,8},{12,10},{14,12},{16,14},{18,... | collective-permute-start | bytes 786440 | tf_op jit(solution)/shard_map/ppermute | solution.py:111
  187.6 3.5 %collective-permute-done.10 = f32[64,1024]{1,0:T(8,128)S(1)} collective-permute-done((f32[64,1024]{1,0:T(8,128)S(1)}, f32[64,1024]{1,0:T(8,128)S(1)}, u32[]{:S(2)}, u32[]{:S(2)}) %collective-permute-start.10) | collective-permute-done | bytes 262176 | tf_op jit(solution)/shard_map/ppermute | solution.py:104
  191.5 4.7 %collective-permute-start.13 = (f32[64,1024]{1,0:T(8,128)S(1)}, f32[64,1024]{1,0:T(8,128)S(1)}, u32[]{:S(2)}, u32[]{:S(2)}) collective-permute-start(f32[64,1024]{1,0:T(8,128)S(1)} %collective-permute-done.11), channel_id=1, source_target_pairs={{0,30},{2,0},{4,2},{6,4},{8,6},{10,8},{12,10},{14,12},{16,14},{18,... | collective-permute-start | bytes 786440 | tf_op jit(solution)/shard_map/ppermute | solution.py:111
  200.1 8.1 %collective-permute-done.14 = f32[64,1024]{1,0:T(8,128)S(1)} collective-permute-done((f32[64,1024]{1,0:T(8,128)S(1)}, f32[64,1024]{1,0:T(8,128)S(1)}, u32[]{:S(2)}, u32[]{:S(2)}) %collective-permute-start.14) | collective-permute-done | bytes 262176 | tf_op jit(solution)/shard_map/ppermute | solution.py:104
  211.1 11.7 %fusion.18 = f32[1024,1024]{1,0:T(8,128)S(1)} fusion(f32[1024,1024]{1,0:T(8,128)} %copy-done, f32[]{:T(128)} %reduce_max.9), kind=kOutput, calls=%fused_computation.24 | convolution fusion | flops 6443499520 | bytes 8388612 | tf_op jit(solution)/shard_map/dot_general | solution.py:33
  222.9 8.6 %add_convert_fusion = bf16[1024,1024]{1,0:T(8,128)(2,1)S(1)} fusion(f32[1024,1024]{1,0:T(8,128)S(1)} %fusion.18, f32[1024,1024]{1,0:T(8,128)S(1)} %copy-done.1, f32[]{:T(128)} %reduce_max.9), kind=kOutput, calls=%fused_computation.8 | convolution fusion | flops 6457131008 | bytes 10485764 | tf_op jit(solution)/shard_map/dot_general | solution.py:35
  231.5 19.6 %multiply_reduce_fusion = (f32[5632]{0:T(1024)S(1)}, f32[1024,5632]{1,0:T(8,128)}) fusion(bf16[1024,1024]{1,0:T(8,128)(2,1)S(1)} %add_convert_fusion, bf16[5632,1024]{1,0:T(8,128)(2,1)} %all-gather.2.cloned.1.call-done), kind=kOutput, calls=%fused_computation.1 | convolution fusion | flops 11822688256 | bytes 36722688 | tf_op jit(solution)/shard_map/dot_general | solution.py:24
  251.1 8.7 %multiply_convert_fusion = bf16[1024,5632]{1,0:T(8,128)(2,1)S(1)} fusion(f32[1024,5632]{1,0:T(8,128)} %get-tuple-element.8, f32[5632]{0:T(1024)S(1)} %add_rsqrt_fusion), kind=kLoop, calls=%fused_computation | loop fusion | flops 11534336 | bytes 34625536 | tf_op jit(solution)/shard_map/convert_element_type | solution.py:25
  259.8 7.7 %fusion.32 = (f32[352]{0:T(512)S(1)}, bf16[352,5632]{1,0:T(8,128)(2,1)}) fusion(bf16[1024,5632]{1,0:T(8,128)(2,1)S(1)} %multiply_convert_fusion, s32[]{:T(128)S(6)} %select_n.160, s32[5632]{0:T(1024)S(1)} %all-reduce, s32[352]{0:T(512)S(1)} %reduce.1), kind=kOutput, calls=%fused_computation.60 | convolution fusion | flops 4073963264 | bytes 16313732 | tf_op jit(solution)/shard_map/dot_general | solution.py:39
  267.6 6.5 %multiply_reduce_fusion.1 = (f32[352]{0:T(512)S(1)}, f32[352,1024]{1,0:T(8,128)S(1)}) fusion(f32[352]{0:T(512)S(1)} %compare_select_fusion, bf16[1024,5632]{1,0:T(8,128)(2,1)S(1)} %multiply_convert_fusion, bf16[352,5632]{1,0:T(8,128)(2,1)} %get-tuple-element.10), kind=kOutput, calls=%fused_computation.26 | convolution fusion | flops 4061167360 | bytes 16943872 | tf_op jit(solution)/shard_map/dot_general | solution.py:44
  (56 shorter events, 16.5 us)
Async XLA Ops:
  6.5 100.7 %all-gather.2.cloned.1.call-start = ((), (), s32[]{:S(2)}) async-start(), calls=%async_computation | async-start | bytes 12255232 | tf_op jit(solution)/shard_map/all_gather | solution.py:85
  7.3 132.0 %all-reduce.3.cloned.1.call-start = ((), (), s32[]{:S(2)}) async-start(), calls=%async_computation.1 | async-start | bytes 524288 | tf_op jit(solution)/shard_map/psum | solution.py:92
  139.3 26.5 %copy-start.2 = (f32[64,1024]{1,0:T(8,128)S(1)}, f32[64,1024]{1,0:T(8,128)}, u32[]{:S(2)}) copy-start(f32[64,1024]{1,0:T(8,128)} %all-reduce.3.cloned.1.call-done) | copy-start | bytes 786436
  139.3 8.8 %collective-permute-start = (f32[64,1024]{1,0:T(8,128)}, f32[64,1024]{1,0:T(8,128)S(1)}, u32[]{:S(2)}, u32[]{:S(2)}) collective-permute-start(f32[64,1024]{1,0:T(8,128)} %all-reduce.3.cloned.1.call-done), channel_id=1, source_target_pairs={{0,2},{2,4},{4,6},{6,8},{8,10},{10,12},{12,14},{14,16},{16,18},{18... | collective-permute-start | bytes 786440 | tf_op jit(solution)/shard_map/ppermute | solution.py:104
  139.3 8.8 %collective-permute-start.1 = (f32[64,1024]{1,0:T(8,128)}, f32[64,1024]{1,0:T(8,128)S(1)}, u32[]{:S(2)}, u32[]{:S(2)}) collective-permute-start(f32[64,1024]{1,0:T(8,128)} %all-reduce.3.cloned.1.call-done), channel_id=1, source_target_pairs={{0,30},{2,0},{4,2},{6,4},{8,6},{10,8},{12,10},{14,12},{16,14},{18,... | collective-permute-start | bytes 786440 | tf_op jit(solution)/shard_map/ppermute | solution.py:111
  148.1 8.6 %collective-permute-start.2 = (f32[64,1024]{1,0:T(8,128)S(1)}, f32[64,1024]{1,0:T(8,128)S(1)}, u32[]{:S(2)}, u32[]{:S(2)}) collective-permute-start(f32[64,1024]{1,0:T(8,128)S(1)} %collective-permute-done), channel_id=1, source_target_pairs={{0,2},{2,4},{4,6},{6,8},{8,10},{10,12},{12,14},{14,16},{16,18},{18... | collective-permute-start | bytes 786440 | tf_op jit(solution)/shard_map/ppermute | solution.py:104
  148.1 8.6 %collective-permute-start.3 = (f32[64,1024]{1,0:T(8,128)S(1)}, f32[64,1024]{1,0:T(8,128)S(1)}, u32[]{:S(2)}, u32[]{:S(2)}) collective-permute-start(f32[64,1024]{1,0:T(8,128)S(1)} %collective-permute-done.1), channel_id=1, source_target_pairs={{0,30},{2,0},{4,2},{6,4},{8,6},{10,8},{12,10},{14,12},{16,14},{18,... | collective-permute-start | bytes 786440 | tf_op jit(solution)/shard_map/ppermute | solution.py:111
  156.7 8.6 %collective-permute-start.4 = (f32[64,1024]{1,0:T(8,128)S(1)}, f32[64,1024]{1,0:T(8,128)S(1)}, u32[]{:S(2)}, u32[]{:S(2)}) collective-permute-start(f32[64,1024]{1,0:T(8,128)S(1)} %collective-permute-done.2), channel_id=1, source_target_pairs={{0,2},{2,4},{4,6},{6,8},{8,10},{10,12},{12,14},{14,16},{16,18},{18... | collective-permute-start | bytes 786440 | tf_op jit(solution)/shard_map/ppermute | solution.py:104
  156.7 9.2 %collective-permute-start.5 = (f32[64,1024]{1,0:T(8,128)S(1)}, f32[64,1024]{1,0:T(8,128)S(1)}, u32[]{:S(2)}, u32[]{:S(2)}) collective-permute-start(f32[64,1024]{1,0:T(8,128)S(1)} %collective-permute-done.3), channel_id=1, source_target_pairs={{0,30},{2,0},{4,2},{6,4},{8,6},{10,8},{12,10},{14,12},{16,14},{18,... | collective-permute-start | bytes 786440 | tf_op jit(solution)/shard_map/ppermute | solution.py:111
  165.3 8.6 %collective-permute-start.6 = (f32[64,1024]{1,0:T(8,128)S(1)}, f32[64,1024]{1,0:T(8,128)S(1)}, u32[]{:S(2)}, u32[]{:S(2)}) collective-permute-start(f32[64,1024]{1,0:T(8,128)S(1)} %collective-permute-done.4), channel_id=1, source_target_pairs={{0,2},{2,4},{4,6},{6,8},{8,10},{10,12},{12,14},{14,16},{16,18},{18... | collective-permute-start | bytes 786440 | tf_op jit(solution)/shard_map/ppermute | solution.py:104
  165.9 8.4 %collective-permute-start.7 = (f32[64,1024]{1,0:T(8,128)S(1)}, f32[64,1024]{1,0:T(8,128)S(1)}, u32[]{:S(2)}, u32[]{:S(2)}) collective-permute-start(f32[64,1024]{1,0:T(8,128)S(1)} %collective-permute-done.5), channel_id=1, source_target_pairs={{0,30},{2,0},{4,2},{6,4},{8,6},{10,8},{12,10},{14,12},{16,14},{18,... | collective-permute-start | bytes 786440 | tf_op jit(solution)/shard_map/ppermute | solution.py:111
  173.9 8.6 %collective-permute-start.8 = (f32[64,1024]{1,0:T(8,128)S(1)}, f32[64,1024]{1,0:T(8,128)S(1)}, u32[]{:S(2)}, u32[]{:S(2)}) collective-permute-start(f32[64,1024]{1,0:T(8,128)S(1)} %collective-permute-done.6), channel_id=1, source_target_pairs={{0,2},{2,4},{4,6},{6,8},{8,10},{10,12},{12,14},{14,16},{16,18},{18... | collective-permute-start | bytes 786440 | tf_op jit(solution)/shard_map/ppermute | solution.py:104
  174.3 8.6 %collective-permute-start.9 = (f32[64,1024]{1,0:T(8,128)S(1)}, f32[64,1024]{1,0:T(8,128)S(1)}, u32[]{:S(2)}, u32[]{:S(2)}) collective-permute-start(f32[64,1024]{1,0:T(8,128)S(1)} %collective-permute-done.7), channel_id=1, source_target_pairs={{0,30},{2,0},{4,2},{6,4},{8,6},{10,8},{12,10},{14,12},{16,14},{18,... | collective-permute-start | bytes 786440 | tf_op jit(solution)/shard_map/ppermute | solution.py:111
  182.5 8.6 %collective-permute-start.10 = (f32[64,1024]{1,0:T(8,128)S(1)}, f32[64,1024]{1,0:T(8,128)S(1)}, u32[]{:S(2)}, u32[]{:S(2)}) collective-permute-start(f32[64,1024]{1,0:T(8,128)S(1)} %collective-permute-done.8), channel_id=1, source_target_pairs={{0,2},{2,4},{4,6},{6,8},{8,10},{10,12},{12,14},{14,16},{16,18},{18... | collective-permute-start | bytes 786440 | tf_op jit(solution)/shard_map/ppermute | solution.py:104
  182.9 8.6 %collective-permute-start.11 = (f32[64,1024]{1,0:T(8,128)S(1)}, f32[64,1024]{1,0:T(8,128)S(1)}, u32[]{:S(2)}, u32[]{:S(2)}) collective-permute-start(f32[64,1024]{1,0:T(8,128)S(1)} %collective-permute-done.9), channel_id=1, source_target_pairs={{0,30},{2,0},{4,2},{6,4},{8,6},{10,8},{12,10},{14,12},{16,14},{18,... | collective-permute-start | bytes 786440 | tf_op jit(solution)/shard_map/ppermute | solution.py:111
  191.1 8.6 %collective-permute-start.12 = (f32[64,1024]{1,0:T(8,128)S(1)}, f32[64,1024]{1,0:T(8,128)S(1)}, u32[]{:S(2)}, u32[]{:S(2)}) collective-permute-start(f32[64,1024]{1,0:T(8,128)S(1)} %collective-permute-done.10), channel_id=1, source_target_pairs={{0,2},{2,4},{4,6},{6,8},{8,10},{10,12},{12,14},{14,16},{16,18},{18... | collective-permute-start | bytes 786440 | tf_op jit(solution)/shard_map/ppermute | solution.py:104
  191.5 8.6 %collective-permute-start.13 = (f32[64,1024]{1,0:T(8,128)S(1)}, f32[64,1024]{1,0:T(8,128)S(1)}, u32[]{:S(2)}, u32[]{:S(2)}) collective-permute-start(f32[64,1024]{1,0:T(8,128)S(1)} %collective-permute-done.11), channel_id=1, source_target_pairs={{0,30},{2,0},{4,2},{6,4},{8,6},{10,8},{12,10},{14,12},{16,14},{18,... | collective-permute-start | bytes 786440 | tf_op jit(solution)/shard_map/ppermute | solution.py:111
  199.7 8.5 %collective-permute-start.14 = (f32[64,1024]{1,0:T(8,128)S(1)}, f32[64,1024]{1,0:T(8,128)S(1)}, u32[]{:S(2)}, u32[]{:S(2)}) collective-permute-start(f32[64,1024]{1,0:T(8,128)S(1)} %collective-permute-done.12), channel_id=1, source_target_pairs={{0,2},{2,4},{4,6},{6,8},{8,10},{10,12},{12,14},{14,16},{16,18},{18... | collective-permute-start | bytes 786440 | tf_op jit(solution)/shard_map/ppermute | solution.py:104
  208.2 1.9 copy-start
  211.1 11.7 %copy-start.1 = (f32[1024,1024]{1,0:T(8,128)S(1)}, f32[1024,1024]{1,0:T(8,128)}, u32[]{:S(2)}) copy-start(f32[1024,1024]{1,0:T(8,128)} %copy-done) | copy-start | bytes 12582916
Sparse Core Ops, SparseCore 0:
  9.6 97.5 all-gather.1
  117.6 21.6 all-reduce.2
